TPU v7x, 256 devices: a whole 4x4x8 slice. The times are simulated.
256 devices in a mesh: rows: 128 (over x, y, z), grp: 2 (over core).
Axes of the slice: x: 4, y: 4, z: 8, core: 2. Of those that a mesh axis runs over, the one named last changes fastest.
Arguments:
- features: float32 [131072, 128], P(('rows', 'grp')), may hold values from -6 to 6
- weight: float32 [128, 256], replicated, may hold values from -0.5 to 0.5
- bias: float32 [256], replicated, may hold values from -3 to 3
- cotangent: float32 [131072, 256], P(('rows', 'grp')), may hold values from -6 to 6
- loc_vals: float32 [131072, 256], P(('rows', 'grp')), may hold values from -0.21875 to 0.21875
- loc_cols: int32 [2048, 4], P(('rows', 'grp')), may hold values from 0 to 7, as said below
- loc_count: int32 [2048], P(('rows', 'grp')), may hold values from 1 to 4, as said below
- hub_rows: int32 [1024], P(('rows', 'grp')), may hold values from 0 to 511, as said below
- hub_vals: float32 [131072, 1024], P(('rows', 'grp')), may hold values from -0.109375 to 0.109375
- send_rows: int32 [256, 128, 4], P(('rows', 'grp')), may hold values from 0 to 511, as said below
- bnd_vals: float32 [131072, 512], P(('rows', 'grp')), may hold values from -0.15625 to 0.15625
Outputs:
- activation: float32 [131072, 256], P(('rows', 'grp'))
- weight_grad: float32 [128, 256], replicated
- feat_grad: float32 [131072, 128], P(('rows', 'grp'))
Inputs may be any that keep to these rules, and one draw needn't show every extreme that they name: `loc_cols`: the 4 listed column tiles of one row tile are distinct. The first loc_count listed tiles of a row tile are live, the others are ignored. `hub_rows`: the 4 hub rows of one device are distinct. `send_rows`: the 4 rows that one device sends to one rows index are distinct.
All inputs are finite; a program needn't handle non-finite values.
Results may differ from a plain program's by a relative error of at most 0.0003.
Values sent between devices are 32-bit elements; how exact they have to be, the bound alone decides.
A program may use at most 64 MiB of HBM per device.

v0:
```python
import jax
import jax.numpy as jnp
from jax import lax
from jax.sharding import PartitionSpec as P

TB = 64
KT = 4


def gelu_tanh(value):
    return jax.nn.gelu(value, approximate=True)


def shards(
    features,
    weight,
    bias,
    cotangent,
    loc_vals,
    loc_cols,
    loc_count,
    hub_rows,
    hub_vals,
    send_rows,
    bnd_vals,
):
    highest = lax.Precision.HIGHEST
    node_dev, width = features.shape
    tiles_dev = node_dev // TB
    blocks = features.reshape(tiles_dev, TB, width)
    local_vals = loc_vals.reshape(tiles_dev, TB, KT, TB)
    live = (jnp.arange(KT, dtype=jnp.int32)[None, :] < loc_count[:, None]).astype(jnp.float32)
    tile_ids = jnp.arange(tiles_dev, dtype=jnp.int32)
    picked = blocks[loc_cols] * live[:, :, None, None]
    local_sum = jnp.einsum("tikj,tkjf->tif", local_vals, picked, precision=highest)
    own_hubs = features[hub_rows]
    cols = hub_vals
    hub_sum = jnp.dot(
        cols, lax.all_gather(own_hubs, ("rows", "grp"), axis=0, tiled=True), precision=highest
    )
    outgoing = features[send_rows[0]]
    incoming = lax.all_to_all(outgoing, "rows", split_axis=0, concat_axis=0, tiled=True)
    bnd_sum = jnp.dot(bnd_vals, incoming.reshape(-1, width), precision=highest)
    aggregated = local_sum.reshape(node_dev, width) + hub_sum + bnd_sum
    pre = jnp.dot(aggregated, weight, precision=highest) + bias
    activation, act_pull = jax.vjp(gelu_tanh, pre)
    pre_grad = act_pull(cotangent)[0]
    total_nodes = node_dev * lax.axis_size("rows") * lax.axis_size("grp")
    weight_term = jnp.dot(aggregated.T, pre_grad, precision=highest)
    weight_grad = lax.psum(weight_term, ("rows", "grp")) * total_nodes ** (-0.5)
    aggregated_grad = jnp.dot(pre_grad, weight.T, precision=highest)
    grad_tiles = aggregated_grad.reshape(tiles_dev, TB, width)
    spread = jnp.einsum("tikj,tif->tkjf", local_vals, grad_tiles, precision=highest)
    spread = spread * live[:, :, None, None]
    one_hot = (loc_cols[:, :, None] == tile_ids[None, None, :]).astype(jnp.float32)
    local_back = jnp.einsum("tks,tkjf->sjf", one_hot, spread, precision=highest)
    cols = hub_vals
    hub_grad = lax.psum_scatter(
        jnp.dot(cols.T, aggregated_grad, precision=highest),
        ("rows", "grp"),
        scatter_dimension=0,
        tiled=True,
    )
    returned = jnp.dot(bnd_vals.T, aggregated_grad, precision=highest).reshape(
        lax.axis_size("rows"), -1, width
    )
    arrived = lax.all_to_all(returned, "rows", split_axis=0, concat_axis=0, tiled=True)
    feat_grad = local_back.reshape(node_dev, width)
    feat_grad = feat_grad.at[hub_rows].add(hub_grad)
    feat_grad = feat_grad.at[send_rows[0].reshape(-1)].add(arrived.reshape(-1, width))
    return (activation, weight_grad, feat_grad)


def solution(mesh):
    return jax.shard_map(
        shards,
        mesh=mesh,
        in_specs=(
            P(("rows", "grp"), None),
            P(),
            P(),
            P(("rows", "grp"), None),
            P(("rows", "grp"), None),
            P(("rows", "grp"), None),
            P(("rows", "grp")),
            P(("rows", "grp")),
            P(("rows", "grp"), None),
            P(("rows", "grp"), None, None),
            P(("rows", "grp"), None),
        ),
        out_specs=(P(("rows", "grp"), None), P(), P(("rows", "grp"), None)),
        check_vma=False,
    )
```

profile of v0, /device:TPU:1, one launch (start us, length us, event | category | flops | bytes accessed | tf_op | source)
XLA Modules:
  0.0 416.0 jit_solution(10820289515364179954)
XLA Ops:
  7.2 0.8 compare_select_fusion.1
  8.0 0.1 copy.32
  8.3 2.6 gather_fusion.2
  10.9 17.0 %all-to-all-start = ((f32[128,4,128]{2,1,0:T(4,128)}), f32[128,4,128]{2,1,0:T(4,128)}, u32[]{:S(2)}, u32[]{:S(2)}) async-start(f32[128,4,128]{2,1,0:T(4,128)} %bitcast.10), calls=%async_computation | async-start | bytes 524288 | tf_op jit(solution)/shard_map/all_to_all | solution.py:42
  27.9 1.4 reshape.111
  29.3 1.5 copy.33
  31.2 1.6 gather_fusion
  32.8 3.9 fusion.3
  36.7 0.1 copy.37
  36.8 1.8 copy.31
  38.6 0.6 gather_fusion.1
  39.3 75.4 %all-gather.1 = f32[256,4,128]{2,1,0:T(4,128)} all-gather(f32[1,4,128]{2,1,0:T(4,128)S(1)} %bitcast.71), channel_id=2, replica_groups=mesh['rows'=128,'grp'=2] {'rows','grp'}, dimensions={0}, use_global_device_ids=true | all-gather | bytes 526336 | tf_op jit(solution)/shard_map/all_gather | solution.py:39
  114.6 2.6 convolution_bitcast_fusion.4
  117.2 3.4 fusion.1
  120.7 1.7 fusion.10
  122.4 1.1 fusion.16
  123.5 0.6 fusion.17
  124.1 2.1 convolution_bitcast_fusion
  126.1 2.7 convolution_bitcast_fusion.3
  128.8 1.8 copy.38
  130.6 10.6 %all-to-all-start.1 = ((f32[128,4,128]{2,1,0:T(4,128)}), f32[128,4,128]{2,1,0:T(4,128)}, u32[]{:S(2)}, u32[]{:S(2)}) async-start(f32[128,4,128]{2,1,0:T(4,128)} %bitcast.70), calls=%async_computation.1 | async-start | bytes 524288 | tf_op jit(solution)/shard_map/all_to_all | solution.py:67
  141.2 0.3 all-reduce.4.cloned.1.call-start
  141.5 0.5 all-reduce.4.cloned.1.call-update
  141.9 1.0 fusion.18
  142.9 0.1 multiply_bitcast_fusion
  143.1 1.5 convolution_bitcast_fusion.1
  144.6 256.7 %all-reduce.4.cloned.1.call-done = (f32[128,256]{1,0:T(8,128)}, f32[1024,128]{0,1:T(8,128)}) async-done(((f32[128,256]{1,0:T(8,128)}, f32[1024,128]{0,1:T(8,128)}), (f32[128,256]{1,0:T(8,128)}, f32[1024,128]{0,1:T(8,128)})) %all-reduce.4.cloned.1.call-update) | async-done | bytes 655376 | tf_op jit(solution)/shard_map/psum | solution.py:50
  401.3 0.9 constant_dynamic-slice_fusion
  402.3 0.8 scatter_fusion
  403.0 1.6 broadcast_multiply_fusion
  404.6 3.8 scatter_fusion.1
  408.4 0.7 copy-done.2
  (38 shorter events, 0.7 us)
Async XLA Ops:
  7.2 110.0 %copy-start = (f32[512,1024]{1,0:T(8,128)S(1)}, f32[512,1024]{1,0:T(8,128)}, u32[]{:S(2)}) copy-start(f32[512,1024]{1,0:T(8,128)} %param.19) | copy-start | bytes 6291460
  7.2 20.7 %copy-start.4 = (f32[512,256]{1,0:T(8,128)S(1)}, f32[512,256]{1,0:T(8,128)}, u32[]{:S(2)}) copy-start(f32[512,256]{1,0:T(8,128)} %param.15) | copy-start | bytes 1572868
  10.9 20.0 %copy-start.8 = (s32[8]{0:T(128)S(1)}, s32[8]{0:T(128)}, u32[]{:S(2)}) copy-start(s32[8]{0:T(128)} %param.17) | copy-start | bytes 100
  10.9 20.1 %copy-start.6 = (s32[8,4]{0,1:T(4,128)S(1)}, s32[8,4]{0,1:T(4,128)}, u32[]{:S(2)}) copy-start(s32[8,4]{0,1:T(4,128)} %param.16) | copy-start | bytes 388
  10.9 20.3 %copy-start.11 = (s32[4]{0:T(128)S(1)}, s32[4]{0:T(128)}, u32[]{:S(2)}) copy-start(s32[4]{0:T(128)} %param.18) | copy-start | bytes 52
  10.9 20.3 %copy-start.1 = (f32[512,128]{1,0:T(8,128)S(1)}, f32[512,128]{1,0:T(8,128)}, u32[]{:S(2)}) copy-start(f32[512,128]{1,0:T(8,128)} %param.11) | copy-start | bytes 786436
  10.9 103.7 %all-to-all-start = ((f32[128,4,128]{2,1,0:T(4,128)}), f32[128,4,128]{2,1,0:T(4,128)}, u32[]{:S(2)}, u32[]{:S(2)}) async-start(f32[128,4,128]{2,1,0:T(4,128)} %bitcast.10), calls=%async_computation | async-start | bytes 524288 | tf_op jit(solution)/shard_map/all_to_all | solution.py:42
  31.2 5.5 %copy-start.7 = (s32[1,128,4]{1,2,0:T(4,128)S(1)}, s32[1,128,4]{1,2,0:T(4,128)}, u32[]{:S(2)}) copy-start(s32[1,128,4]{1,2,0:T(4,128)} %param.20) | copy-start | bytes 6148
  39.1 78.1 %copy-start.3 = (f32[512,128]{0,1:T(8,128)S(1)}, f32[512,128]{0,1:T(8,128)}, u32[]{:S(2)}) copy-start(f32[512,128]{0,1:T(8,128)} %copy.31) | copy-start | bytes 786436
  117.2 3.5 copy-start.5
  117.2 3.5 copy-start.9
  117.2 3.5 copy-start.10
  130.6 274.0 %all-to-all-start.1 = ((f32[128,4,128]{2,1,0:T(4,128)}), f32[128,4,128]{2,1,0:T(4,128)}, u32[]{:S(2)}, u32[]{:S(2)}) async-start(f32[128,4,128]{2,1,0:T(4,128)} %bitcast.70), calls=%async_computation.1 | async-start | bytes 524288 | tf_op jit(solution)/shard_map/all_to_all | solution.py:67
  141.2 260.1 %all-reduce.4.cloned.1.call-start = ((), (), s32[]{:S(2)}) async-start(), calls=%async_computation.2 | async-start | bytes 1310720 | tf_op jit(solution)/shard_map/psum | solution.py:50
  408.4 0.7 copy-start.2
Sparse Core Ops, SparseCore 0:
  148.2 253.0 all-reduce.3
where the time goes:
time: 417 us; the launch traced here: 416 us
  waiting for transfers between devices  257 us (62%)
  blocking collectives  75.4 us (18%)
  starting transfers between devices  27.8 us (7%)
  matrix products  20.4 us (5%)
  between operations  14.3 us (3%)
  local copies, waits for them, and re-layouts  13.7 us (3%)
  other arithmetic  7.22 us (2%)
    psum x1, waiting for transfers between devices, shards(): weight_grad = lax.psum(weight_term, ('rows', 'grp')) * total_nodes ** (-0.5)  257 us
    all_gather x1, blocking collectives, shards(): lax.all_gather(own_hubs, ('rows', 'grp'), axis=0, tiled=True)  75.4 us
    all_to_all x1, starting transfers between devices, shards(): lax.all_to_all(outgoing, 'rows', split_axis=0, concat_axis=0, tiled=True)  17 us
    all_to_all x1, starting transfers between devices, shards(): lax.all_to_all(returned, 'rows', split_axis=0, concat_axis=0, tiled=True)  10.6 us
  transfers between devices with their start and end apart: 3, of which 1 were waited for; matrix products, arithmetic and copies ran while one was open for 4% of the time, Pallas kernels for 0%

commit v1 on v0

v1 whole, which is shorter than its diff:
```python
import functools
import math

import jax
import jax.numpy as jnp
from jax import lax
from jax.experimental import pallas as pl
from jax.experimental.pallas import tpu as pltpu
from jax.sharding import PartitionSpec as P

TB = 64
KT = 4
MESH = pl.DeviceIdType.MESH
F32 = jnp.float32
BF16 = jnp.bfloat16
C0 = math.sqrt(2.0 / math.pi)
C1 = 0.044715


def split(value):
    high = value.astype(BF16)
    low = (value - high.astype(F32)).astype(BF16)
    return high, low


def mm(left, right):
    return jnp.dot(left, right, preferred_element_type=F32)


def wide(value):
    high, low = split(value)
    return jnp.concatenate([high, low], axis=1)


def mm3(high, low, pair):
    n = pair.shape[1] // 2
    both = mm(high, pair)
    return both[:, :n] + both[:, n:] + mm(low, pair[:, :n])


def kernel(
    XY, Z,
    feat_h, w_h, b_h, cot_h, lv_h, lcols_h, lcount_h, hrows_h, hv_h, srows_h, bv_h,
    act_o, wg_o, fg_o,
    feat, w, b, cot, lv, lcols, lcount, hrows, hrows_v, hv, srows, srows_v, bv,
    ahi, alo, athi, atlo, wt, wpair,
    hown, s1, r1, h1, br, hub,
    agg, prg, dag,
    gs, gsib, gown, gx, gp, gz,
    bsend, bx, ar,
    ws, wx, wp, wz, wsum, wsib, wall,
    in_sem, loc_sem, ssem, rsem,
):
    r = lax.axis_index("rows")
    g = lax.axis_index("grp")
    xy = r // Z
    z = lax.rem(r, Z)
    half = Z // 2
    R = XY * Z
    F = feat.shape[1]
    N = feat.shape[0]
    nb = bv.shape[1]
    nh = hv.shape[1]
    hb = half * 8

    loads = {}
    for i, (name, src, dst) in enumerate([
        ("feat", feat_h, feat), ("srows", srows_h, srows), ("hrows", hrows_h, hrows),
        ("lcols", lcols_h, lcols), ("lcount", lcount_h, lcount),
        ("lv", lv_h, lv), ("bv", bv_h, bv), ("hv", hv_h, hv), ("w", w_h, w), ("b", b_h, b),
        ("cot", cot_h, cot), ("srows_v", srows_h, srows_v), ("hrows_v", hrows_h, hrows_v),
    ]):
        loads[name] = pltpu.make_async_copy(src, dst, in_sem.at[i])
        loads[name].start()

    barrier = pltpu.get_barrier_semaphore()

    def zpeer(i):
        return xy * Z + lax.rem(z + i, Z)

    def xypeer(i):
        return lax.rem(xy + i, XY) * Z + z

    def signal(dev, core):
        pl.semaphore_signal(barrier, inc=1, device_id=(dev, core), device_id_type=MESH)

    def sig_z(i, c):
        signal(zpeer(i), g)
        signal(zpeer(i), 1 - g)
        return c

    def sig_xy(i, c):
        signal(xypeer(i), g)
        return c

    lax.fori_loop(1, Z, sig_z, 0)
    lax.fori_loop(1, XY, sig_xy, 0)
    signal(r, 1 - g)

    loads["feat"].wait()
    loads["srows"].wait()
    loads["hrows"].wait()

    def pack(i, c):
        slot = lax.rem(i, Z) * XY + i // Z
        for j in range(4):
            s1[slot, pl.ds(j, 1), :] = feat[pl.ds(srows[0, i * 4 + j], 1), :]
        return c

    lax.fori_loop(0, R, pack, 0, unroll=4)
    for j in range(4):
        hown[pl.ds(j, 1), :] = feat[pl.ds(hrows[0, j], 1), :]

    pl.semaphore_wait(barrier, 2 * (Z - 1) + (XY - 1) + 1)

    def remote(src, dst, k, dev, core):
        return pltpu.make_async_remote_copy(
            src_ref=src, dst_ref=dst, send_sem=ssem.at[k], recv_sem=rsem.at[k],
            device_id=(dev, core), device_id_type=MESH)

    def wait_recv(ref, k):
        pltpu.make_async_copy(ref, ref, rsem.at[k]).wait()

    def wait_send(ref, k):
        pltpu.make_async_copy(ref, ref, ssem.at[k]).wait()

    def send_hub_z(i, c):
        remote(hown, h1.at[z], 0, zpeer(i), g).start()
        return c

    def send_bnd_z(i, c):
        p = lax.rem(z + i, Z)
        remote(s1.at[pl.ds(p * XY, XY)], r1.at[z], 1, zpeer(i), g).start()
        return c

    lax.fori_loop(1, Z, send_hub_z, 0)
    pltpu.make_async_copy(hown, h1.at[z], rsem.at[0]).start()
    lax.fori_loop(1, Z, send_bnd_z, 0)
    pltpu.make_async_copy(s1.at[pl.ds(z * XY, XY)], r1.at[z], rsem.at[1]).start()

    loads["lcols"].wait()
    loads["lcount"].wait()
    loads["lv"].wait()
    lane = lax.broadcasted_iota(jnp.int32, (TB, 2 * TB), 1)
    upper = lane >= TB
    for t in range(N // TB):
        rows = pl.ds(t * TB, TB)
        dup = []
        for pair in range(KT // 2):
            v = lv[rows, pl.ds(pair * 2 * TB, 2 * TB)]
            turned = pltpu.roll(v, TB, 1)
            dup.append(jnp.where(upper, turned, v))
            dup.append(jnp.where(upper, v, turned))
        cols = [jnp.where(k < lcount[0, t], lcols[0, t * KT + k], -1) for k in range(KT)]
        for c in range(N // (2 * TB)):
            tile = jnp.where(upper, 2 * c + 1, 2 * c)
            out = jnp.zeros((TB, 2 * TB), F32)
            for k in range(KT):
                out = jnp.where(tile == cols[k], dup[k], out)
            high, low = split(out)
            ahi[rows, pl.ds(c * 2 * TB, 2 * TB)] = high
            alo[rows, pl.ds(c * 2 * TB, 2 * TB)] = low

    wait_recv(h1, 0)

    def send_hub_xy(i, c):
        remote(h1, hub.at[g, pl.ds(xy * Z, Z)], 2, xypeer(i), g).start()
        return c

    lax.fori_loop(1, XY, send_hub_xy, 0)
    pltpu.make_async_copy(h1, hub.at[g, pl.ds(xy * Z, Z)], rsem.at[2]).start()

    wait_recv(r1, 1)

    def send_bnd_xy(i, c):
        remote(r1.at[:, lax.rem(xy + i, XY)], br.at[pl.ds(xy * Z, Z)], 3, xypeer(i), g).start()
        return c

    lax.fori_loop(1, XY, send_bnd_xy, 0)
    pltpu.make_async_copy(r1.at[:, xy], br.at[pl.ds(xy * Z, Z)], rsem.at[3]).start()

    agg[...] = mm3(ahi[:, :N], alo[:, :N], wide(feat[...]))
    for c in range(N // 128):
        cols = pl.ds(c * 128, 128)
        athi[cols, :] = ahi[:, cols].astype(F32).T.astype(BF16)
        atlo[cols, :] = alo[:, cols].astype(F32).T.astype(BF16)

    loads["w"].wait()
    wv = w[...]
    wpair[...] = wide(wv)
    wt[...] = wide(wv.T)

    loads["bv"].wait()
    step = min(128, nb)
    for c in range(nb // step):
        v = bv[:, pl.ds(c * step, step)]
        high, low = split(v)
        ahi[:, pl.ds(N + c * step, step)] = high
        alo[:, pl.ds(N + c * step, step)] = low
        high, low = split(v.T)
        athi[pl.ds(N + c * step, step), :] = high
        atlo[pl.ds(N + c * step, step), :] = low

    loads["hv"].wait()
    step = min(128, nh)
    for c in range(nh // step):
        v = hv[:, pl.ds(c * step, step)]
        high, low = split(v)
        ahi[:, pl.ds(N + nb + c * step, step)] = high
        alo[:, pl.ds(N + nb + c * step, step)] = low
        high, low = split(v.T)
        for q in range(step // hb):
            block = c * (step // hb) + q
            to = N + nb + (block % 2) * (nh // 2) + (block // 2) * hb
            athi[pl.ds(to, hb), :] = high[q * hb:(q + 1) * hb]
            atlo[pl.ds(to, hb), :] = low[q * hb:(q + 1) * hb]

    wait_recv(hub.at[g], 2)
    to_sib = remote(hub.at[g], hub.at[g], 4, r, 1 - g)
    to_sib.start()
    wait_recv(br, 3)
    vb = br[...].reshape(nb, F)
    agg[...] += mm3(ahi[:, N:N + nb], alo[:, N:N + nb], wide(vb))
    to_sib.wait_recv()
    vh = jnp.concatenate([hub[0], hub[1]], axis=1).reshape(nh, F)
    agg[...] += mm3(ahi[:, N + nb:], alo[:, N + nb:], wide(vh))

    loads["b"].wait()
    loads["cot"].wait()
    H = w.shape[1]
    step = 128
    wsplit = wpair[...]
    for c in range(N // step):
        rows = pl.ds(c * step, step)
        high, low = split(agg[rows, :])
        both = mm(high, wsplit)
        v = both[:, :H] + both[:, H:] + mm(low, wsplit[:, :H]) + b[...]
        sq = v * v
        t = jnp.tanh(C0 * (v + C1 * (sq * v)))
        act_o[rows, :] = 0.5 * v * (1.0 + t)
        slope = 0.5 * (1.0 + t) + 0.5 * v * (1.0 - t * t) * (C0 * (1.0 + 3.0 * C1 * sq))
        prg[rows, :] = cot[rows, :] * slope
    high, low = split(prg[...])
    dag[...] = wide(mm3(high, low, wt[...]))

    g2 = dag[...]

    def back(start, size):
        return mm3(athi[pl.ds(start, size), :], atlo[pl.ds(start, size), :], g2)

    hbase = N + nb
    gs[...] = back(hbase + (1 - g) * (nh // 2), nh // 2)
    hub_sib = remote(gs, gsib, 5, r, 1 - g)
    hub_sib.start()
    bsend[...] = back(N, nb).reshape(R, 4, F)

    def bback_xy(i, c):
        p = lax.rem(xy + i, XY)
        remote(bsend.at[pl.ds(p * Z, Z)], bx.at[xy], 6, xypeer(i), g).start()
        return c

    lax.fori_loop(1, XY, bback_xy, 0)
    pltpu.make_async_copy(bsend.at[pl.ds(xy * Z, Z)], bx.at[xy], rsem.at[6]).start()

    own = back(hbase + g * (nh // 2), nh // 2)
    hub_sib.wait_recv()
    gown[...] = (own + gsib[...]).reshape(XY, hb, F)

    def hback_xy(i, c):
        remote(gown.at[lax.rem(xy + i, XY)], gx.at[xy], 7, xypeer(i), g).start()
        return c

    lax.fori_loop(1, XY, hback_xy, 0)
    pltpu.make_async_copy(gown.at[xy], gx.at[xy], rsem.at[7]).start()

    ag_t = agg[...].T
    ahigh, alow = split(ag_t)
    p2 = prg[...]
    wh, wl = split(p2)
    wterm = mm(ahigh, wh) + mm(ahigh, wl) + mm(alow, wh)
    piece = ws.shape[1]
    ws[...] = jnp.concatenate([wterm[:, :F], wterm[:, F:]], axis=0).reshape(XY, piece, F)

    def wxy(i, c):
        remote(ws.at[lax.rem(xy + i, XY)], wx.at[xy], 8, xypeer(i), g).start()
        return c

    lax.fori_loop(1, XY, wxy, 0)
    pltpu.make_async_copy(ws.at[xy], wx.at[xy], rsem.at[8]).start()

    fg_o[...] = back(0, N)

    wait_recv(bx, 6)

    def bback_z(i, c):
        p = lax.rem(z + i, Z)
        remote(bx.at[:, p], ar.at[z], 9, zpeer(i), g).start()
        return c

    lax.fori_loop(1, Z, bback_z, 0)
    pltpu.make_async_copy(bx.at[:, z], ar.at[z], rsem.at[9]).start()

    wait_recv(gx, 7)
    total = gx[0]
    for i in range(1, XY):
        total += gx[i]
    gp[...] = total.reshape(half, 8, F)

    for i in range(half):
        zi = half * g + i
        for core in range(2):
            mine = (zi == z) & (core == g)

            @pl.when(jnp.logical_not(mine))
            def _():
                remote(gp.at[i], gz.at[z], 10, xy * Z + zi, core).start()

            @pl.when(mine)
            def _():
                pltpu.make_async_copy(gp.at[i], gz.at[z], rsem.at[10]).start()

    wait_recv(wx, 8)
    total = wx[0]
    for i in range(1, XY):
        total += wx[i]
    wp[...] = total

    def wzs(i, c):
        remote(wp, wz.at[z], 11, zpeer(i), g).start()
        return c

    lax.fori_loop(1, Z, wzs, 0)
    pltpu.make_async_copy(wp, wz.at[z], rsem.at[11]).start()
    wait_recv(wz, 11)
    total = wz[0]
    for i in range(1, Z):
        total += wz[i]
    wsum[0] = total
    w_sib = remote(wsum.at[0], wsib, 12, r, 1 - g)
    w_sib.start()
    w_sib.wait_recv()
    wsum[1] = total + wsib[...]

    def wag(i, c):
        remote(wsum.at[1], wall.at[xy], 13, xypeer(i), g).start()
        return c

    lax.fori_loop(1, XY, wag, 0)
    pltpu.make_async_copy(wsum.at[1], wall.at[xy], rsem.at[13]).start()

    loads["srows_v"].wait()
    loads["hrows_v"].wait()
    node = lax.broadcasted_iota(jnp.int32, (N, nb), 0)
    pick = jnp.where(node == srows_v[...], 1.0, 0.0).astype(BF16)
    wait_recv(ar, 9)
    arr = jnp.concatenate([ar[i] for i in range(Z)], axis=1).reshape(nb, F)
    both = mm(pick, wide(arr))
    fg_o[...] += both[:, :F] + both[:, F:]

    wait_recv(gz, 10)
    total = gz[0]
    for i in range(1, Z):
        total += gz[i]
    node = lax.broadcasted_iota(jnp.int32, (N, F), 0)
    for j in range(4):
        row = jnp.where(g == 0, total[j:j + 1, :], total[4 + j:5 + j, :])
        fg_o[...] += jnp.where(node == hrows[0, j], row, 0.0)

    wait_recv(wall, 13)
    full = wall[...].reshape(2 * F, F) * float((R * 2 * N) ** -0.5)
    wg_o[:, :F] = full[:F]
    wg_o[:, F:] = full[F:]

    wait_send(h1.at[pl.ds(0, Z - 1)], 0)
    wait_send(s1.at[pl.ds(0, (Z - 1) * XY)], 1)
    wait_send(hub.at[0, pl.ds(0, (XY - 1) * Z)], 2)
    wait_send(br.at[pl.ds(0, (XY - 1) * Z)], 3)
    to_sib.wait_send()
    hub_sib.wait_send()
    wait_send(bsend.at[pl.ds(0, (XY - 1) * Z)], 6)
    wait_send(gown.at[pl.ds(0, XY - 1)], 7)
    wait_send(ws.at[pl.ds(0, XY - 1)], 8)
    wait_send(ar.at[pl.ds(0, Z - 1)], 9)

    @pl.when(z // half == g)
    def _():
        wait_send(gz.at[pl.ds(0, 2 * half - 1)], 10)

    @pl.when(z // half != g)
    def _():
        wait_send(gz.at[pl.ds(0, 2 * half)], 10)

    wait_send(wz.at[pl.ds(0, Z - 1)], 11)
    w_sib.wait_send()
    wait_send(wall.at[pl.ds(0, XY - 1)], 13)


def shards(features, weight, bias, cotangent, loc_vals, loc_cols, loc_count, hub_rows, hub_vals, send_rows, bnd_vals):
    rows = lax.axis_size("rows")
    Z = 8 if rows % 8 == 0 else 2
    XY = rows // Z
    N, F = features.shape
    H = weight.shape[1]
    nb = bnd_vals.shape[1]
    nh = hub_vals.shape[1]
    half = Z // 2
    hb = half * 8
    piece = 2 * F // XY
    K = N + nb + nh
    V = pltpu.VMEM
    D = pltpu.SemaphoreType.DMA
    any_ = pl.BlockSpec(memory_space=pl.ANY)
    vm = pl.BlockSpec(memory_space=pltpu.VMEM)
    scratch = [
        V((N, F), F32), V((F, H), F32), V((1, H), F32), V((N, H), F32), V((N, KT * TB), F32),
        pltpu.SMEM((1, N // TB * KT), jnp.int32), pltpu.SMEM((1, N // TB), jnp.int32),
        pltpu.SMEM((1, 4), jnp.int32), V((1, 4), jnp.int32),
        V((N, nh), F32), pltpu.SMEM((1, nb), jnp.int32), V((1, nb), jnp.int32), V((N, nb), F32),
        V((N, K), BF16), V((N, K), BF16), V((K, N), BF16), V((K, N), BF16),
        V((H, 2 * F), BF16), V((F, 2 * H), BF16),
        V((4, F), F32), V((rows, 4, F), F32), V((Z, XY, 4, F), F32), V((Z, 4, F), F32),
        V((rows, 4, F), F32), V((2, rows, 4, F), F32),
        V((N, F), F32), V((N, H), F32), V((N, 2 * F), BF16),
        V((nh // 2, F), F32), V((nh // 2, F), F32), V((XY, hb, F), F32), V((XY, hb, F), F32),
        V((half, 8, F), F32), V((Z, 8, F), F32),
        V((rows, 4, F), F32), V((XY, Z, 4, F), F32), V((Z, XY, 4, F), F32),
        V((XY, piece, F), F32), V((XY, piece, F), F32), V((piece, F), F32), V((Z, piece, F), F32),
        V((2, piece, F), F32), V((piece, F), F32), V((XY, piece, F), F32),
        D((13,)), D((1,)), D((14,)), D((14,)),
    ]
    return pl.pallas_call(
        functools.partial(kernel, XY, Z),
        out_shape=(
            jax.ShapeDtypeStruct((N, H), F32),
            jax.ShapeDtypeStruct((F, H), F32),
            jax.ShapeDtypeStruct((N, F), F32),
        ),
        in_specs=[any_] * 11,
        out_specs=(vm, vm, vm),
        scratch_shapes=scratch,
        compiler_params=pltpu.CompilerParams(
            collective_id=0, has_side_effects=True, vmem_limit_bytes=48 * 1024 * 1024
        ),
    )(
        features, weight, bias.reshape(1, H), cotangent, loc_vals, loc_cols.reshape(1, -1),
        loc_count.reshape(1, -1), hub_rows.reshape(1, 4), hub_vals,
        send_rows.reshape(1, nb), bnd_vals,
    )


def solution(mesh):
    node = P(("rows", "grp"), None)
    flat = P(("rows", "grp"))
    return jax.shard_map(
        shards,
        mesh=mesh,
        in_specs=(node, P(), P(), node, node, node, flat, flat, node, P(("rows", "grp"), None, None), node),
        out_specs=(node, P(), node),
        check_vma=False,
    )
```

time: 417 us -> 64.8 us (0.16)
  waiting for transfers between devices: 257 us -> 0 us
  blocking collectives: 75.4 us -> 0 us
  Pallas kernels: 0 us -> 51.1 us
  starting transfers between devices: 27.8 us -> 0 us
  matrix products: 20.4 us -> 0 us
  between operations: 14.3 us -> 0.66 us
  other arithmetic: 7.22 us -> 0 us
    psum x1 -> x0, waiting for transfers between devices: 257 us -> none  [shards(): weight_grad = lax.psum(weight_term, ('rows', 'grp')) * total_nodes ** (-0.5)]
    all_gather x1 -> x0, blocking collectives: 75.4 us -> none  [shards(): lax.all_gather(own_hubs, ('rows', 'grp'), axis=0, tiled=True)]
    pallas_call x0 -> x1, Pallas kernels: none -> 51.1 us  [shards(): pl.pallas_call(functools.partial(kernel, XY, Z), out_shape=(jax.ShapeDtyp...]
    all_to_all x2 -> x0, starting transfers between devices: 27.6 us -> none  [the longest x1 17 us: shards(): lax.all_to_all(outgoing, 'rows', split_axis=0, concat_axis=0, tiled=True)]
    dot_general x9 -> x0, matrix products: 19.4 us -> none  [the longest x1 3.86 us: shards(): jnp.einsum('tikj,tkjf->tif', local_vals, picked, precision=highest)]
    unnamed x26 -> x23, local copies, waits for them, and re-layouts: 1.78 us -> 12.4 us
    gather x3 -> x0, local copies, waits for them, and re-layouts: 4.74 us -> none  [the longest x1 2.59 us: shards(): outgoing = features[send_rows[0]]]
    reshape x3 -> x2, local copies, waits for them, and re-layouts: 4.76 us -> 0.19 us  [the longest x1 0.11 us: shards(): send_rows.reshape(1, nb)]
  transfers between devices with their start and end apart: 3 -> 0, of which waited for: 1 -> 0; matrix products, arithmetic and copies ran while one was open for 4% -> 0% of each run, Pallas kernels for 0% -> 0%
where the time goes in v1:
time: 64.8 us; the launch traced here: 64.4 us
  Pallas kernels  51.1 us (79%)
  local copies, waits for them, and re-layouts  12.6 us (19%)
  between operations  0.66 us (1%)
    pallas_call x1, Pallas kernels, shards(): pl.pallas_call(functools.partial(kernel, XY, Z), out_shape=(jax.ShapeDtyp...  51.1 us
    unnamed x23, local copies, waits for them, and re-layouts  12.4 us

profile of v1, /device:TPU:1, one launch (start us, length us, event | category | flops | bytes accessed | tf_op | source)
XLA Modules:
  0.0 64.4 jit_solution(14410792307762953316)
XLA Ops:
  0.6 0.8 %copy.16 = s32[8,4]{1,0:T(8,128)S(1)} copy(s32[8,4]{0,1:T(4,128)} %param.16) | data formatting | bytes 256 | tf_op args[5]
  1.4 0.1 reshape.22.lcols_h
  1.5 0.8 %copy.17 = s32[1,128,4]{2,1,0:T(8,128)S(1)} copy(s32[1,128,4]{1,2,0:T(4,128)} %param.20) | data formatting | bytes 4096 | tf_op args[9]
  2.3 0.1 reshape.25.srows_h
  2.4 0.0 copy-start
  2.4 1.6 %copy-done = f32[512,1024]{1,0:T(8,128)S(1)} copy-done((f32[512,1024]{1,0:T(8,128)S(1)}, f32[512,1024]{1,0:T(8,128)}, u32[]{:S(2)}) %copy-start) | copy-done | bytes 2097176
  4.0 0.0 copy-start.1
  4.0 1.2 %copy-done.1 = f32[512,512]{1,0:T(8,128)S(1)} copy-done((f32[512,512]{1,0:T(8,128)S(1)}, f32[512,512]{1,0:T(8,128)}, u32[]{:S(2)}) %copy-start.1) | copy-done | bytes 1048600
  5.2 0.0 copy-start.2
  5.2 1.0 %copy-done.2 = f32[512,256]{1,0:T(8,128)S(1)} copy-done((f32[512,256]{1,0:T(8,128)S(1)}, f32[512,256]{1,0:T(8,128)}, u32[]{:S(2)}) %copy-start.2) | copy-done | bytes 524312
  6.2 0.0 copy-start.3
  6.2 1.0 %copy-done.3 = f32[512,256]{1,0:T(8,128)S(1)} copy-done((f32[512,256]{1,0:T(8,128)S(1)}, f32[512,256]{1,0:T(8,128)}, u32[]{:S(2)}) %copy-start.3) | copy-done | bytes 524312
  7.3 0.0 copy-start.4
  7.3 0.9 %copy-done.4 = f32[512,128]{1,0:T(8,128)S(1)} copy-done((f32[512,128]{1,0:T(8,128)S(1)}, f32[512,128]{1,0:T(8,128)}, u32[]{:S(2)}) %copy-start.4) | copy-done | bytes 262168
  8.2 0.0 copy-start.5
  8.2 0.9 %copy-done.5 = f32[128,256]{1,0:T(8,128)S(1)} copy-done((f32[128,256]{1,0:T(8,128)S(1)}, f32[128,256]{1,0:T(8,128)}, u32[]{:S(2)}) %copy-start.5) | copy-done | bytes 131096
  9.1 0.0 copy-start.6
  9.1 0.7 %copy-done.6 = f32[256]{0:T(256)S(1)} copy-done((f32[256]{0:T(256)S(1)}, f32[256]{0:T(256)}, u32[]{:S(2)}) %copy-start.6) | copy-done | bytes 1048
  9.8 0.0 copy-start.7
  9.8 0.7 %copy-done.7 = s32[8]{0:T(128)S(1)} copy-done((s32[8]{0:T(128)S(1)}, s32[8]{0:T(128)}, u32[]{:S(2)}) %copy-start.7) | copy-done | bytes 56
  10.5 0.0 copy-start.8
  10.5 0.7 %copy-done.8 = s32[4]{0:T(128)S(1)} copy-done((s32[4]{0:T(128)S(1)}, s32[4]{0:T(128)}, u32[]{:S(2)}) %copy-start.8) | copy-done | bytes 40
  11.1 51.1 %shard_map.130 = (f32[512,256]{1,0:T(8,128)S(1)}, f32[128,256]{1,0:T(8,128)S(1)}, f32[512,128]{1,0:T(8,128)S(1)}) custom-call(f32[512,128]{1,0:T(8,128)S(1)} %copy-done.4, f32[128,256]{1,0:T(8,128)S(1)} %copy-done.5, f32[1,256]{1,0:T(1,128)S(1)} %bitcast.3, f32[512,256]{1,0:T(8,128)S(1)} %copy-done.2, f32[512,256]{1,0:T(8,128)S(1)} %copy-done.3, ...), custom_call_target="tpu_custom_call" | custom-call | tf_op jit(solution)/shard_map/pallas_call | solution.py:431
  62.2 0.8 %copy.21 = f32[512,256]{1,0:T(8,128)} copy(f32[512,256]{1,0:T(8,128)S(1)} %get-tuple-element.6) | data formatting | bytes 1048576
  63.0 0.7 %copy.22 = f32[128,256]{1,0:T(8,128)} copy(f32[128,256]{1,0:T(8,128)S(1)} %get-tuple-element.7) | data formatting | bytes 262144
  63.7 0.7 %copy.23 = f32[512,128]{1,0:T(8,128)} copy(f32[512,128]{1,0:T(8,128)S(1)} %get-tuple-element.8) | data formatting | bytes 524288
Async XLA Ops:
  2.4 1.6 %copy-start = (f32[512,1024]{1,0:T(8,128)S(1)}, f32[512,1024]{1,0:T(8,128)}, u32[]{:S(2)}) copy-start(f32[512,1024]{1,0:T(8,128)} %hv_h.1) | copy-start | bytes 6291460
  4.0 1.2 %copy-start.1 = (f32[512,512]{1,0:T(8,128)S(1)}, f32[512,512]{1,0:T(8,128)}, u32[]{:S(2)}) copy-start(f32[512,512]{1,0:T(8,128)} %bv_h.1) | copy-start | bytes 3145732
  5.2 1.0 %copy-start.2 = (f32[512,256]{1,0:T(8,128)S(1)}, f32[512,256]{1,0:T(8,128)}, u32[]{:S(2)}) copy-start(f32[512,256]{1,0:T(8,128)} %cot_h.1) | copy-start | bytes 1572868
  6.2 1.0 %copy-start.3 = (f32[512,256]{1,0:T(8,128)S(1)}, f32[512,256]{1,0:T(8,128)}, u32[]{:S(2)}) copy-start(f32[512,256]{1,0:T(8,128)} %lv_h.1) | copy-start | bytes 1572868
  7.3 0.9 %copy-start.4 = (f32[512,128]{1,0:T(8,128)S(1)}, f32[512,128]{1,0:T(8,128)}, u32[]{:S(2)}) copy-start(f32[512,128]{1,0:T(8,128)} %feat_h.1) | copy-start | bytes 786436
  8.2 0.9 %copy-start.5 = (f32[128,256]{1,0:T(8,128)S(1)}, f32[128,256]{1,0:T(8,128)}, u32[]{:S(2)}) copy-start(f32[128,256]{1,0:T(8,128)} %w_h.1) | copy-start | bytes 393220
  9.1 0.7 %copy-start.6 = (f32[256]{0:T(256)S(1)}, f32[256]{0:T(256)}, u32[]{:S(2)}) copy-start(f32[256]{0:T(256)} %param.13) | copy-start | bytes 3076
  9.8 0.7 %copy-start.7 = (s32[8]{0:T(128)S(1)}, s32[8]{0:T(128)}, u32[]{:S(2)}) copy-start(s32[8]{0:T(128)} %param.17) | copy-start | bytes 100
  10.5 0.7 %copy-start.8 = (s32[4]{0:T(128)S(1)}, s32[4]{0:T(128)}, u32[]{:S(2)}) copy-start(s32[4]{0:T(128)} %param.18) | copy-start | bytes 52

commit v2 on v1

v2 whole, which is shorter than its diff:
```python
import functools
import math

import jax
import jax.numpy as jnp
from jax import lax
from jax.experimental import pallas as pl
from jax.experimental.pallas import tpu as pltpu
from jax.sharding import PartitionSpec as P

TB = 64
KT = 4
MESH = pl.DeviceIdType.MESH
F32 = jnp.float32
BF16 = jnp.bfloat16
C0 = math.sqrt(2.0 / math.pi)
C1 = 0.044715


def split(value):
    high = value.astype(BF16)
    low = (value - high.astype(F32)).astype(BF16)
    return high, low


def mm(left, right):
    return jnp.dot(left, right, preferred_element_type=F32)


def wide(value):
    high, low = split(value)
    return jnp.concatenate([high, low], axis=1)


def mm3(high, low, pair):
    n = pair.shape[1] // 2
    both = mm(high, pair)
    return both[:, :n] + both[:, n:] + mm(low, pair[:, :n])


def kernel(
    X, Y, Z,
    feat_h, w_h, b_h, cot_h, lv_h, lcols_h, lcount_h, hrows_h, hv_h, srows_h, bv_h,
    act_o, wg_o, fg_o,
    feat, w, b, cot, lv, lcols, lcount, hrows, hv, srows, srows_v, bv,
    ahi, alo, athi, atlo, wt, wpair,
    hown, s1, h1, br, hub,
    agg, prg, dag,
    gs, gsib, gown, gx, gp, gz,
    bsend, ar,
    ws, wx, wp, wz, wsum, wall,
    in_sem, ssem, rsem, plane_sem,
):
    r = lax.axis_index("rows")
    g = lax.axis_index("grp")
    xy = r // Z
    z = lax.rem(r, Z)
    half = Z // 2
    XY = X * Y
    R = XY * Z
    F = feat.shape[1]
    N = feat.shape[0]
    nb = bv.shape[1]
    nh = hv.shape[1]
    hb = half * 8

    loads = {}

    def load(*names):
        for name in names:
            src, dst, i = arrays[name]
            loads[name] = pltpu.make_async_copy(src, dst, in_sem.at[i])
            loads[name].start()

    arrays = {}
    for i, (name, src, dst) in enumerate([
        ("feat", feat_h, feat), ("srows", srows_h, srows), ("hrows", hrows_h, hrows),
        ("lcols", lcols_h, lcols), ("lcount", lcount_h, lcount),
        ("lv", lv_h, lv), ("bv", bv_h, bv), ("hv", hv_h, hv), ("w", w_h, w), ("b", b_h, b),
        ("cot", cot_h, cot), ("srows_v", srows_h, srows_v),
    ]):
        arrays[name] = (src, dst, i)
    load("srows", "hrows", "feat")

    barrier = pltpu.get_barrier_semaphore()
    x = xy // Y
    y = lax.rem(xy, Y)
    z_order = sorted(range(1, Z), key=lambda d: -min(d, Z - d))
    xy_order = sorted(
        ((dx, dy) for dx in range(X) for dy in range(Y)),
        key=lambda d: -min(d[0], X - d[0]) - min(d[1], Y - d[1]))[:-1]

    def zline(d):
        return lax.rem(z + d, Z)

    def plane(d):
        return lax.rem(x + d[0], X) * Y + lax.rem(y + d[1], Y)

    def signal(sem, dev, core):
        pl.semaphore_signal(sem, inc=1, device_id=(dev, core), device_id_type=MESH)

    for d in z_order:
        signal(barrier, xy * Z + zline(d), g)
    for d in xy_order:
        signal(barrier, plane(d) * Z + z, g)
    for d in z_order:
        signal(barrier, xy * Z + zline(d), 1 - g)
    for d in xy_order:
        signal(barrier, plane(d) * Z + z, 1 - g)
    signal(barrier, r, 1 - g)
    load("lcols", "lcount", "lv", "w", "b", "srows_v")

    loads["srows"].wait()
    loads["hrows"].wait()
    loads["feat"].wait()

    def pack(i, c):
        for j in range(4):
            s1[i, pl.ds(j, 1), :] = feat[pl.ds(srows[j, i], 1), :]
        return c

    for j in range(4):
        hown[pl.ds(j, 1), :] = feat[pl.ds(hrows[0, j], 1), :]
    lax.fori_loop(0, R, pack, 0, unroll=4)
    load("bv", "hv", "cot")

    pl.semaphore_wait(barrier, 2 * (Z - 1) + 2 * (XY - 1) + 1)

    for d in z_order:
        signal(plane_sem, xy * Z + zline(d), g)

    def remote(src, dst, k, dev, core):
        return pltpu.make_async_remote_copy(
            src_ref=src, dst_ref=dst, send_sem=ssem.at[k], recv_sem=rsem.at[k],
            device_id=(dev, core), device_id_type=MESH)

    def wait_recv(ref, k):
        pltpu.make_async_copy(ref, ref, rsem.at[k]).wait()

    def wait_send(ref, k):
        pltpu.make_async_copy(ref, ref, ssem.at[k]).wait()

    def each(order, send):
        def step(d, k, c):
            back = (k + 1) // 2
            dz = lax.rem(Z // 2 + lax.rem(k, 2) * (Z - 2 * back) + back, Z)
            send(plane(d) * Z + zline(dz))
            return c

        for d in order:
            lax.fori_loop(0, Z, functools.partial(step, d), 0)

    def rest(send):
        for d in z_order:
            send(xy * Z + zline(d))

    first, second = xy_order[:len(xy_order) // 2], xy_order[len(xy_order) // 2:]

    def send_bnd(p):
        remote(s1.at[p], br.at[r], 3, p, g).start()

    for d in z_order:
        remote(hown, h1.at[z], 0, xy * Z + zline(d), g).start()
    pltpu.make_async_copy(hown, h1.at[z], rsem.at[0]).start()
    pltpu.make_async_copy(s1.at[r], br.at[r], rsem.at[3]).start()
    wait_recv(h1, 0)
    for d in xy_order:
        remote(h1, hub.at[g, pl.ds(xy * Z, Z)], 2, plane(d) * Z + z, g).start()
    pltpu.make_async_copy(h1, hub.at[g, pl.ds(xy * Z, Z)], rsem.at[2]).start()
    pl.semaphore_wait(plane_sem, Z - 1)
    each(first + second, send_bnd)
    rest(send_bnd)

    loads["lcols"].wait()
    loads["lcount"].wait()
    loads["lv"].wait()
    lane = lax.broadcasted_iota(jnp.int32, (TB, 2 * TB), 1)
    upper = lane >= TB
    for t in range(N // TB):
        rows = pl.ds(t * TB, TB)
        dup = []
        for pair in range(KT // 2):
            v = lv[rows, pl.ds(pair * 2 * TB, 2 * TB)]
            turned = pltpu.roll(v, TB, 1)
            dup.append(jnp.where(upper, turned, v))
            dup.append(jnp.where(upper, v, turned))
        cols = [jnp.where(k < lcount[0, t], lcols[k, t], -1) for k in range(KT)]
        for c in range(N // (2 * TB)):
            tile = jnp.where(upper, 2 * c + 1, 2 * c)
            out = jnp.zeros((TB, 2 * TB), F32)
            for k in range(KT):
                out = jnp.where(tile == cols[k], dup[k], out)
            high, low = split(out)
            ahi[rows, pl.ds(c * 2 * TB, 2 * TB)] = high
            alo[rows, pl.ds(c * 2 * TB, 2 * TB)] = low

    agg[...] = mm3(ahi[:, :N], alo[:, :N], wide(feat[...]))
    for c in range(N // 128):
        cols = pl.ds(c * 128, 128)
        athi[cols, :] = ahi[:, cols].astype(F32).T.astype(BF16)
        atlo[cols, :] = alo[:, cols].astype(F32).T.astype(BF16)

    loads["w"].wait()
    wv = w[...]
    wpair[...] = wide(wv)
    wt[...] = wide(wv.T)

    loads["bv"].wait()
    step = min(128, nb)
    for c in range(nb // step):
        v = bv[:, pl.ds(c * step, step)]
        high, low = split(v)
        ahi[:, pl.ds(N + c * step, step)] = high
        alo[:, pl.ds(N + c * step, step)] = low
        high, low = split(v.T)
        athi[pl.ds(N + c * step, step), :] = high
        atlo[pl.ds(N + c * step, step), :] = low

    loads["hv"].wait()
    step = min(128, nh)
    for c in range(nh // step):
        v = hv[:, pl.ds(c * step, step)]
        high, low = split(v)
        ahi[:, pl.ds(N + nb + c * step, step)] = high
        alo[:, pl.ds(N + nb + c * step, step)] = low
        high, low = split(v.T)
        for q in range(step // hb):
            block = c * (step // hb) + q
            to = N + nb + (block % 2) * (nh // 2) + (block // 2) * hb
            athi[pl.ds(to, hb), :] = high[q * hb:(q + 1) * hb]
            atlo[pl.ds(to, hb), :] = low[q * hb:(q + 1) * hb]

    wait_recv(hub.at[g], 2)
    to_sib = remote(hub.at[g], hub.at[g], 4, r, 1 - g)
    to_sib.start()
    wait_recv(br, 3)
    vb = br[...].reshape(nb, F)
    agg[...] += mm3(ahi[:, N:N + nb], alo[:, N:N + nb], wide(vb))
    to_sib.wait_recv()
    vh = jnp.concatenate([hub[0], hub[1]], axis=1).reshape(nh, F)
    agg[...] += mm3(ahi[:, N + nb:], alo[:, N + nb:], wide(vh))

    loads["b"].wait()
    loads["cot"].wait()
    H = w.shape[1]
    step = 128
    wsplit = wpair[...]
    for c in range(N // step):
        rows = pl.ds(c * step, step)
        high, low = split(agg[rows, :])
        both = mm(high, wsplit)
        v = both[:, :H] + both[:, H:] + mm(low, wsplit[:, :H]) + b[...]
        sq = v * v
        t = jnp.tanh(C0 * (v + C1 * (sq * v)))
        act_o[rows, :] = 0.5 * v * (1.0 + t)
        slope = 0.5 * (1.0 + t) + 0.5 * v * (1.0 - t * t) * (C0 * (1.0 + 3.0 * C1 * sq))
        prg[rows, :] = cot[rows, :] * slope
    ahigh, alow = split(agg[...].T)
    wh, wl = split(prg[...])
    wterm = mm(ahigh, wh) + mm(ahigh, wl) + mm(alow, wh)
    piece = ws.shape[2]
    ws[...] = jnp.concatenate([wterm[:, :F], wterm[:, F:]], axis=0).reshape(XY, 2, piece, F)

    for d in xy_order:
        for core in (g, 1 - g):
            remote(ws.at[plane(d), core], wx.at[xy * 2 + g], 8, plane(d) * Z + z, core).start()
    remote(ws.at[xy, 1 - g], wx.at[xy * 2 + g], 8, r, 1 - g).start()
    pltpu.make_async_copy(ws.at[xy, g], wx.at[xy * 2 + g], rsem.at[8]).start()

    high, low = split(prg[...])
    dag[...] = wide(mm3(high, low, wt[...]))

    g2 = dag[...]

    def back(start, size):
        return mm3(athi[pl.ds(start, size), :], atlo[pl.ds(start, size), :], g2)

    hbase = N + nb
    gs[...] = back(hbase + (1 - g) * (nh // 2), nh // 2)
    hub_sib = remote(gs, gsib, 5, r, 1 - g)
    hub_sib.start()
    bsend[...] = back(N, nb).reshape(R, 4, F)

    def send_back(p):
        remote(bsend.at[p], ar.at[r], 6, p, g).start()

    pltpu.make_async_copy(bsend.at[r], ar.at[r], rsem.at[6]).start()
    each(first, send_back)

    own = back(hbase + g * (nh // 2), nh // 2)
    hub_sib.wait_recv()
    gown[...] = (own + gsib[...]).reshape(XY, hb, F)
    for d in xy_order:
        remote(gown.at[plane(d)], gx.at[xy], 7, plane(d) * Z + z, g).start()
    pltpu.make_async_copy(gown.at[xy], gx.at[xy], rsem.at[7]).start()

    wait_recv(wx, 8)
    total = wx[0]
    for i in range(1, 2 * XY):
        total += wx[i]
    wp[...] = total
    for d in z_order:
        remote(wp, wz.at[z], 11, xy * Z + zline(d), g).start()
    pltpu.make_async_copy(wp, wz.at[z], rsem.at[11]).start()

    each(second, send_back)
    rest(send_back)

    wait_recv(gx, 7)
    total = gx[0]
    for i in range(1, XY):
        total += gx[i]
    gp[...] = total.reshape(half, 8, F)

    for i in range(half):
        zi = half * g + i
        for core in range(2):
            mine = (zi == z) & (core == g)

            @pl.when(jnp.logical_not(mine))
            def _():
                remote(gp.at[i], gz.at[z], 10, xy * Z + zi, core).start()

            @pl.when(mine)
            def _():
                pltpu.make_async_copy(gp.at[i], gz.at[z], rsem.at[10]).start()

    fg_o[...] = back(0, N)

    wait_recv(wz, 11)
    total = wz[0]
    for i in range(1, Z):
        total += wz[i]
    wsum[...] = total

    for d in xy_order:
        for core in (g, 1 - g):
            remote(wsum, wall.at[xy * 2 + g], 13, plane(d) * Z + z, core).start()
    remote(wsum, wall.at[xy * 2 + g], 13, r, 1 - g).start()
    pltpu.make_async_copy(wsum, wall.at[xy * 2 + g], rsem.at[13]).start()

    loads["srows_v"].wait()
    node = lax.broadcasted_iota(jnp.int32, (N, R), 0)
    picks = [jnp.where(node == srows_v[pl.ds(j, 1), :], 1.0, 0.0).astype(BF16) for j in range(4)]
    pick = jnp.concatenate(picks, axis=1)
    wait_recv(ar, 6)
    arr = jnp.concatenate([ar[:, j, :] for j in range(4)], axis=0)
    both = mm(pick, wide(arr))
    fg_o[...] += both[:, :F] + both[:, F:]

    wait_recv(gz, 10)
    total = gz[0]
    for i in range(1, Z):
        total += gz[i]
    node = lax.broadcasted_iota(jnp.int32, (N, F), 0)
    for j in range(4):
        row = jnp.where(g == 0, total[j:j + 1, :], total[4 + j:5 + j, :])
        fg_o[...] += jnp.where(node == hrows[0, j], row, 0.0)

    wait_recv(wall, 13)
    full = wall[...].reshape(2 * F, F) * float((R * 2 * N) ** -0.5)
    wg_o[:, :F] = full[:F]
    wg_o[:, F:] = full[F:]

    wait_send(h1.at[pl.ds(0, Z - 1)], 0)
    wait_send(hub.at[0, pl.ds(0, (XY - 1) * Z)], 2)
    wait_send(br.at[pl.ds(0, R - 1)], 3)
    to_sib.wait_send()
    hub_sib.wait_send()
    wait_send(ar.at[pl.ds(0, R - 1)], 6)
    wait_send(gown.at[pl.ds(0, XY - 1)], 7)
    wait_send(wx.at[pl.ds(0, 2 * XY - 1)], 8)

    @pl.when(z // half == g)
    def _():
        wait_send(gz.at[pl.ds(0, 2 * half - 1)], 10)

    @pl.when(z // half != g)
    def _():
        wait_send(gz.at[pl.ds(0, 2 * half)], 10)

    wait_send(wz.at[pl.ds(0, Z - 1)], 11)
    wait_send(wall.at[pl.ds(0, 2 * XY - 1)], 13)


def write_out(a_ref, b_ref, c_ref, a_out, b_out, c_out, sems):
    copies = [
        pltpu.make_async_copy(a_ref, a_out, sems.at[0]),
        pltpu.make_async_copy(b_ref, b_out, sems.at[1]),
        pltpu.make_async_copy(c_ref, c_out, sems.at[2]),
    ]
    for copy in copies:
        copy.start()
    for copy in copies:
        copy.wait()


def shards(features, weight, bias, cotangent, loc_vals, loc_cols, loc_count, hub_rows, hub_vals, send_rows, bnd_vals):
    rows = lax.axis_size("rows")
    Z = 8 if rows % 8 == 0 else 2
    XY = rows // Z
    Y = 4 if XY % 4 == 0 else 1
    X = XY // Y
    N, F = features.shape
    H = weight.shape[1]
    nb = bnd_vals.shape[1]
    nh = hub_vals.shape[1]
    half = Z // 2
    hb = half * 8
    piece = F // XY
    K = N + nb + nh
    V = pltpu.VMEM
    D = pltpu.SemaphoreType.DMA
    hbm = pl.BlockSpec(memory_space=pltpu.HBM)
    vm = pl.BlockSpec(memory_space=pltpu.VMEM)
    scratch = [
        V((N, F), F32), V((F, H), F32), V((1, H), F32), V((N, H), F32), V((N, KT * TB), F32),
        pltpu.SMEM((KT, N // TB), jnp.int32), pltpu.SMEM((1, N // TB), jnp.int32),
        pltpu.SMEM((1, 4), jnp.int32),
        V((N, nh), F32), pltpu.SMEM((4, rows), jnp.int32), V((4, rows), jnp.int32), V((N, nb), F32),
        V((N, K), BF16), V((N, K), BF16), V((K, N), BF16), V((K, N), BF16),
        V((H, 2 * F), BF16), V((F, 2 * H), BF16),
        V((4, F), F32), V((rows, 4, F), F32), V((Z, 4, F), F32),
        V((rows, 4, F), F32), V((2, rows, 4, F), F32),
        V((N, F), F32), V((N, H), F32), V((N, 2 * F), BF16),
        V((nh // 2, F), F32), V((nh // 2, F), F32), V((XY, hb, F), F32), V((XY, hb, F), F32),
        V((half, 8, F), F32), V((Z, 8, F), F32),
        V((rows, 4, F), F32), V((rows, 4, F), F32),
        V((XY, 2, piece, F), F32), V((2 * XY, piece, F), F32), V((piece, F), F32), V((Z, piece, F), F32),
        V((piece, F), F32), V((2 * XY, piece, F), F32),
        D((12,)), D((14,)), D((14,)), pltpu.SemaphoreType.REGULAR,
    ]
    results = pl.pallas_call(
        functools.partial(kernel, X, Y, Z),
        out_shape=(pltpu.VMEM((N, H), F32), pltpu.VMEM((F, H), F32), pltpu.VMEM((N, F), F32)),
        in_specs=[hbm] * 11,
        out_specs=(vm, vm, vm),
        scratch_shapes=scratch,
        compiler_params=pltpu.CompilerParams(
            collective_id=0, has_side_effects=True, vmem_limit_bytes=60 * 1024 * 1024
        ),
    )(
        features, weight, bias.reshape(1, H), cotangent, loc_vals, loc_cols.T,
        loc_count.reshape(1, -1), hub_rows.reshape(1, 4), hub_vals,
        send_rows[0].T, bnd_vals,
    )
    return pl.pallas_call(
        write_out,
        out_shape=(
            jax.ShapeDtypeStruct((N, H), F32),
            jax.ShapeDtypeStruct((F, H), F32),
            jax.ShapeDtypeStruct((N, F), F32),
        ),
        in_specs=[vm] * 3,
        out_specs=(pl.BlockSpec(memory_space=pl.ANY),) * 3,
        scratch_shapes=[D((3,))],
        compiler_params=pltpu.CompilerParams(vmem_limit_bytes=4 * 1024 * 1024),
    )(*results)


def solution(mesh):
    node = P(("rows", "grp"), None)
    flat = P(("rows", "grp"))
    return jax.shard_map(
        shards,
        mesh=mesh,
        in_specs=(node, P(), P(), node, node, node, flat, flat, node, P(("rows", "grp"), None, None), node),
        out_specs=(node, P(), node),
        check_vma=False,
    )
```

time: 64.8 us -> 44 us (0.68)
  local copies, waits for them, and re-layouts: 12.6 us -> 0 us
  Pallas kernels: 51.1 us -> 43.2 us
    unnamed x23 -> x0, local copies, waits for them, and re-layouts: 12.4 us -> none
    pallas_call x1 -> x2, Pallas kernels: 51.1 us -> 43.2 us  [the longest x1 42.3 us: shards(): pl.pallas_call(functools.partial(kernel, X, Y, Z), out_shape=(pltpu.VMEM(...]
where the time goes in v2:
time: 44 us; the launch traced here: 43.9 us
  Pallas kernels  43.2 us (98%)
  between operations  0.64 us (1%)
    pallas_call x1, Pallas kernels, shards(): pl.pallas_call(functools.partial(kernel, X, Y, Z), out_shape=(pltpu.VMEM(...  42.3 us
    pallas_call x1, Pallas kernels, shards(): pl.pallas_call(write_out, out_shape=(jax.ShapeDtypeStruct((N, H), F32), j...  0.95 us

profile of v2, /device:TPU:1, one launch (start us, length us, event | category | flops | bytes accessed | tf_op | source)
XLA Modules:
  0.0 43.9 jit_solution(7949734893937777546)
XLA Ops:
  0.6 42.3 %shard_map.130 = (f32[512,256]{1,0:T(8,128)S(1)}, f32[128,256]{1,0:T(8,128)S(1)}, f32[512,128]{1,0:T(8,128)S(1)}) custom-call(f32[512,128]{1,0:T(8,128)} %feat_h.1, f32[128,256]{1,0:T(8,128)} %w_h.1, f32[1,256]{1,0:T(1,128)} %bitcast.9, f32[512,256]{1,0:T(8,128)} %cot_h.1, f32[512,256]{1,0:T(8,128)} %lv_h.1, s32[4,8]{1,0:T(4,128)} %bitcast.7, ...), custom_call_target="tpu_custom_call" | custom-call | tf_op jit(solution)/shard_map/pallas_call | solution.py:433
  42.9 0.9 %shard_map.131 = (f32[512,256]{1,0:T(8,128)}, f32[128,256]{1,0:T(8,128)}, f32[512,128]{1,0:T(8,128)}) custom-call(f32[512,256]{1,0:T(8,128)S(1)} %get-tuple-element.6.a_ref, f32[128,256]{1,0:T(8,128)S(1)} %get-tuple-element.7.b_ref, f32[512,128]{1,0:T(8,128)S(1)} %get-tuple-element.8.c_ref), custom_call_target="tpu_custom_call" | custom-call | tf_op jit(solution)/shard_map/pallas_call | solution.py:447

commit v3 on v2

--- a/solution.py
+++ b/solution.py
@@ -48,21 +48,20 @@
     agg, prg, dag,
     gs, gsib, gown, gx, gp, gz,
     bsend, ar,
-    ws, wx, wp, wz, wsum, wall,
+    ws, wx, wp, wsib, wz, wsum, wall,
     in_sem, ssem, rsem, plane_sem,
 ):
     r = lax.axis_index("rows")
     g = lax.axis_index("grp")
     xy = r // Z
     z = lax.rem(r, Z)
-    half = Z // 2
     XY = X * Y
     R = XY * Z
     F = feat.shape[1]
     N = feat.shape[0]
     nb = bv.shape[1]
     nh = hv.shape[1]
-    hb = half * 8
+    hb = Z * 4
 
     loads = {}
 
@@ -103,31 +102,18 @@
         signal(barrier, xy * Z + zline(d), g)
     for d in xy_order:
         signal(barrier, plane(d) * Z + z, g)
-    for d in z_order:
-        signal(barrier, xy * Z + zline(d), 1 - g)
-    for d in xy_order:
-        signal(barrier, plane(d) * Z + z, 1 - g)
     signal(barrier, r, 1 - g)
     load("lcols", "lcount", "lv", "w", "b", "srows_v")
 
-    loads["srows"].wait()
     loads["hrows"].wait()
     loads["feat"].wait()
-
-    def pack(i, c):
-        for j in range(4):
-            s1[i, pl.ds(j, 1), :] = feat[pl.ds(srows[j, i], 1), :]
-        return c
-
     for j in range(4):
         hown[pl.ds(j, 1), :] = feat[pl.ds(hrows[0, j], 1), :]
-    lax.fori_loop(0, R, pack, 0, unroll=4)
-    load("bv", "hv", "cot")
-
-    pl.semaphore_wait(barrier, 2 * (Z - 1) + 2 * (XY - 1) + 1)
+
+    pl.semaphore_wait(barrier, (Z - 1) + (XY - 1) + 1)
 
     for d in z_order:
-        signal(plane_sem, xy * Z + zline(d), g)
+        signal(plane_sem.at[z], xy * Z + zline(d), g)
 
     def remote(src, dst, k, dev, core):
         return pltpu.make_async_remote_copy(
@@ -162,14 +148,30 @@
     for d in z_order:
         remote(hown, h1.at[z], 0, xy * Z + zline(d), g).start()
     pltpu.make_async_copy(hown, h1.at[z], rsem.at[0]).start()
+
+    loads["srows"].wait()
+
+    def pack(i, c):
+        for j in range(4):
+            s1[i, pl.ds(j, 1), :] = feat[pl.ds(srows[j, i], 1), :]
+        return c
+
+    lax.fori_loop(0, R, pack, 0, unroll=4)
+    load("bv", "hv", "cot")
     pltpu.make_async_copy(s1.at[r], br.at[r], rsem.at[3]).start()
+    for d in xy_order:
+        send_bnd(plane(d) * Z + z)
+
+    for pair in range(1, Z // 2 + 1):
+        for d in sorted({pair, Z - pair}):
+            pl.semaphore_wait(plane_sem.at[zline(d)], 1)
+        for dxy in xy_order + [(0, 0)]:
+            for d in sorted({pair, Z - pair}):
+                send_bnd(plane(dxy) * Z + zline(d))
     wait_recv(h1, 0)
     for d in xy_order:
         remote(h1, hub.at[g, pl.ds(xy * Z, Z)], 2, plane(d) * Z + z, g).start()
     pltpu.make_async_copy(h1, hub.at[g, pl.ds(xy * Z, Z)], rsem.at[2]).start()
-    pl.semaphore_wait(plane_sem, Z - 1)
-    each(first + second, send_bnd)
-    rest(send_bnd)
 
     loads["lcols"].wait()
     loads["lcount"].wait()
@@ -223,22 +225,22 @@
         high, low = split(v)
         ahi[:, pl.ds(N + nb + c * step, step)] = high
         alo[:, pl.ds(N + nb + c * step, step)] = low
-        high, low = split(v.T)
-        for q in range(step // hb):
-            block = c * (step // hb) + q
-            to = N + nb + (block % 2) * (nh // 2) + (block // 2) * hb
-            athi[pl.ds(to, hb), :] = high[q * hb:(q + 1) * hb]
-            atlo[pl.ds(to, hb), :] = low[q * hb:(q + 1) * hb]
+        turned = v.T.reshape(step // 8, 8, N)
+        for core in range(2):
+            high, low = split(turned[:, core * 4:core * 4 + 4, :].reshape(step // 2, N))
+            to = pl.ds(N + nb + core * (nh // 2) + c * (step // 2), step // 2)
+            athi[to, :] = high
+            atlo[to, :] = low
 
     wait_recv(hub.at[g], 2)
     to_sib = remote(hub.at[g], hub.at[g], 4, r, 1 - g)
     to_sib.start()
+    to_sib.wait_recv()
+    vh = jnp.concatenate([hub[0], hub[1]], axis=1).reshape(nh, F)
+    agg[...] += mm3(ahi[:, N + nb:], alo[:, N + nb:], wide(vh))
     wait_recv(br, 3)
     vb = br[...].reshape(nb, F)
     agg[...] += mm3(ahi[:, N:N + nb], alo[:, N:N + nb], wide(vb))
-    to_sib.wait_recv()
-    vh = jnp.concatenate([hub[0], hub[1]], axis=1).reshape(nh, F)
-    agg[...] += mm3(ahi[:, N + nb:], alo[:, N + nb:], wide(vh))
 
     loads["b"].wait()
     loads["cot"].wait()
@@ -258,14 +260,10 @@
     ahigh, alow = split(agg[...].T)
     wh, wl = split(prg[...])
     wterm = mm(ahigh, wh) + mm(ahigh, wl) + mm(alow, wh)
-    piece = ws.shape[2]
-    ws[...] = jnp.concatenate([wterm[:, :F], wterm[:, F:]], axis=0).reshape(XY, 2, piece, F)
-
-    for d in xy_order:
-        for core in (g, 1 - g):
-            remote(ws.at[plane(d), core], wx.at[xy * 2 + g], 8, plane(d) * Z + z, core).start()
-    remote(ws.at[xy, 1 - g], wx.at[xy * 2 + g], 8, r, 1 - g).start()
-    pltpu.make_async_copy(ws.at[xy, g], wx.at[xy * 2 + g], rsem.at[8]).start()
+    ws[...] = jnp.concatenate([wterm[:, :F], wterm[:, F:]], axis=0).reshape(ws.shape)
+    for d in xy_order:
+        remote(ws.at[plane(d)], wx.at[xy], 8, plane(d) * Z + z, g).start()
+    pltpu.make_async_copy(ws.at[xy], wx.at[xy], rsem.at[8]).start()
 
     high, low = split(prg[...])
     dag[...] = wide(mm3(high, low, wt[...]))
@@ -279,7 +277,13 @@
     gs[...] = back(hbase + (1 - g) * (nh // 2), nh // 2)
     hub_sib = remote(gs, gsib, 5, r, 1 - g)
     hub_sib.start()
+    own = back(hbase + g * (nh // 2), nh // 2)
     bsend[...] = back(N, nb).reshape(R, 4, F)
+    hub_sib.wait_recv()
+    gown[...] = (own + gsib[...]).reshape(XY, hb, F)
+    for d in xy_order:
+        remote(gown.at[plane(d)], gx.at[xy], 7, plane(d) * Z + z, g).start()
+    pltpu.make_async_copy(gown.at[xy], gx.at[xy], rsem.at[7]).start()
 
     def send_back(p):
         remote(bsend.at[p], ar.at[r], 6, p, g).start()
@@ -287,45 +291,32 @@
     pltpu.make_async_copy(bsend.at[r], ar.at[r], rsem.at[6]).start()
     each(first, send_back)
 
-    own = back(hbase + g * (nh // 2), nh // 2)
-    hub_sib.wait_recv()
-    gown[...] = (own + gsib[...]).reshape(XY, hb, F)
-    for d in xy_order:
-        remote(gown.at[plane(d)], gx.at[xy], 7, plane(d) * Z + z, g).start()
-    pltpu.make_async_copy(gown.at[xy], gx.at[xy], rsem.at[7]).start()
-
     wait_recv(wx, 8)
     total = wx[0]
-    for i in range(1, 2 * XY):
+    for i in range(1, XY):
         total += wx[i]
-    wp[...] = total
+    wp[0] = total
+    w_sib = remote(wp.at[0], wsib, 12, r, 1 - g)
+    w_sib.start()
+    w_sib.wait_recv()
+    wp[1] = total + wsib[...]
     for d in z_order:
-        remote(wp, wz.at[z], 11, xy * Z + zline(d), g).start()
-    pltpu.make_async_copy(wp, wz.at[z], rsem.at[11]).start()
+        remote(wp.at[1], wz.at[z], 11, xy * Z + zline(d), g).start()
+    pltpu.make_async_copy(wp.at[1], wz.at[z], rsem.at[11]).start()
 
     each(second, send_back)
     rest(send_back)
+
+    fg_o[...] = back(0, N)
 
     wait_recv(gx, 7)
     total = gx[0]
     for i in range(1, XY):
         total += gx[i]
-    gp[...] = total.reshape(half, 8, F)
-
-    for i in range(half):
-        zi = half * g + i
-        for core in range(2):
-            mine = (zi == z) & (core == g)
-
-            @pl.when(jnp.logical_not(mine))
-            def _():
-                remote(gp.at[i], gz.at[z], 10, xy * Z + zi, core).start()
-
-            @pl.when(mine)
-            def _():
-                pltpu.make_async_copy(gp.at[i], gz.at[z], rsem.at[10]).start()
-
-    fg_o[...] = back(0, N)
+    gp[...] = total.reshape(Z, 4, F)
+    for d in z_order:
+        remote(gp.at[zline(d)], gz.at[z], 10, xy * Z + zline(d), g).start()
+    pltpu.make_async_copy(gp.at[z], gz.at[z], rsem.at[10]).start()
 
     wait_recv(wz, 11)
     total = wz[0]
@@ -334,10 +325,8 @@
     wsum[...] = total
 
     for d in xy_order:
-        for core in (g, 1 - g):
-            remote(wsum, wall.at[xy * 2 + g], 13, plane(d) * Z + z, core).start()
-    remote(wsum, wall.at[xy * 2 + g], 13, r, 1 - g).start()
-    pltpu.make_async_copy(wsum, wall.at[xy * 2 + g], rsem.at[13]).start()
+        remote(wsum, wall.at[xy], 13, plane(d) * Z + z, g).start()
+    pltpu.make_async_copy(wsum, wall.at[xy], rsem.at[13]).start()
 
     loads["srows_v"].wait()
     node = lax.broadcasted_iota(jnp.int32, (N, R), 0)
@@ -354,8 +343,7 @@
         total += gz[i]
     node = lax.broadcasted_iota(jnp.int32, (N, F), 0)
     for j in range(4):
-        row = jnp.where(g == 0, total[j:j + 1, :], total[4 + j:5 + j, :])
-        fg_o[...] += jnp.where(node == hrows[0, j], row, 0.0)
+        fg_o[...] += jnp.where(node == hrows[0, j], total[j:j + 1, :], 0.0)
 
     wait_recv(wall, 13)
     full = wall[...].reshape(2 * F, F) * float((R * 2 * N) ** -0.5)
@@ -369,18 +357,12 @@
     hub_sib.wait_send()
     wait_send(ar.at[pl.ds(0, R - 1)], 6)
     wait_send(gown.at[pl.ds(0, XY - 1)], 7)
-    wait_send(wx.at[pl.ds(0, 2 * XY - 1)], 8)
-
-    @pl.when(z // half == g)
-    def _():
-        wait_send(gz.at[pl.ds(0, 2 * half - 1)], 10)
-
-    @pl.when(z // half != g)
-    def _():
-        wait_send(gz.at[pl.ds(0, 2 * half)], 10)
-
+    wait_send(wx.at[pl.ds(0, XY - 1)], 8)
+
+    wait_send(gz.at[pl.ds(0, Z - 1)], 10)
     wait_send(wz.at[pl.ds(0, Z - 1)], 11)
-    wait_send(wall.at[pl.ds(0, 2 * XY - 1)], 13)
+    w_sib.wait_send()
+    wait_send(wall.at[pl.ds(0, XY - 1)], 13)
 
 
 def write_out(a_ref, b_ref, c_ref, a_out, b_out, c_out, sems):
@@ -405,9 +387,8 @@
     H = weight.shape[1]
     nb = bnd_vals.shape[1]
     nh = hub_vals.shape[1]
-    half = Z // 2
-    hb = half * 8
-    piece = F // XY
+    hb = Z * 4
+    piece = 2 * F // XY
     K = N + nb + nh
     V = pltpu.VMEM
     D = pltpu.SemaphoreType.DMA
@@ -424,11 +405,11 @@
         V((rows, 4, F), F32), V((2, rows, 4, F), F32),
         V((N, F), F32), V((N, H), F32), V((N, 2 * F), BF16),
         V((nh // 2, F), F32), V((nh // 2, F), F32), V((XY, hb, F), F32), V((XY, hb, F), F32),
-        V((half, 8, F), F32), V((Z, 8, F), F32),
+        V((Z, 4, F), F32), V((Z, 4, F), F32),
         V((rows, 4, F), F32), V((rows, 4, F), F32),
-        V((XY, 2, piece, F), F32), V((2 * XY, piece, F), F32), V((piece, F), F32), V((Z, piece, F), F32),
-        V((piece, F), F32), V((2 * XY, piece, F), F32),
-        D((12,)), D((14,)), D((14,)), pltpu.SemaphoreType.REGULAR,
+        V((XY, piece, F), F32), V((XY, piece, F), F32), V((2, piece, F), F32), V((piece, F), F32),
+        V((Z, piece, F), F32), V((piece, F), F32), V((XY, piece, F), F32),
+        D((12,)), D((14,)), D((14,)), pltpu.SemaphoreType.REGULAR((Z,)),
     ]
     results = pl.pallas_call(
         functools.partial(kernel, X, Y, Z),

time: 44 us -> 41.3 us (0.939)
  Pallas kernels: 43.2 us -> 40.6 us
    pallas_call x1, Pallas kernels: 42.3 us -> 39.6 us  [shards(): pl.pallas_call(functools.partial(kernel, X, Y, Z), out_shape=(pltpu.VMEM(...]
where the time goes in v3:
time: 41.3 us; the launch traced here: 41.2 us
  Pallas kernels  40.6 us (98%)
  between operations  0.64 us (2%)
    pallas_call x1, Pallas kernels, shards(): pl.pallas_call(functools.partial(kernel, X, Y, Z), out_shape=(pltpu.VMEM(...  39.6 us
    pallas_call x1, Pallas kernels, shards(): pl.pallas_call(write_out, out_shape=(jax.ShapeDtypeStruct((N, H), F32), j...  0.95 us

profile of v3, /device:TPU:1, one launch (start us, length us, event | category | flops | bytes accessed | tf_op | source)
XLA Modules:
  0.0 41.2 jit_solution(17334363416854887647)
XLA Ops:
  0.6 39.6 %shard_map.130 = (f32[512,256]{1,0:T(8,128)S(1)}, f32[128,256]{1,0:T(8,128)S(1)}, f32[512,128]{1,0:T(8,128)S(1)}) custom-call(f32[512,128]{1,0:T(8,128)} %feat_h.1, f32[128,256]{1,0:T(8,128)} %w_h.1, f32[1,256]{1,0:T(1,128)} %bitcast.9, f32[512,256]{1,0:T(8,128)} %cot_h.1, f32[512,256]{1,0:T(8,128)} %lv_h.1, s32[4,8]{1,0:T(4,128)} %bitcast.7, ...), custom_call_target="tpu_custom_call" | custom-call | tf_op jit(solution)/shard_map/pallas_call | solution.py:414
  40.3 0.9 %shard_map.131 = (f32[512,256]{1,0:T(8,128)}, f32[128,256]{1,0:T(8,128)}, f32[512,128]{1,0:T(8,128)}) custom-call(f32[512,256]{1,0:T(8,128)S(1)} %get-tuple-element.6.a_ref, f32[128,256]{1,0:T(8,128)S(1)} %get-tuple-element.7.b_ref, f32[512,128]{1,0:T(8,128)S(1)} %get-tuple-element.8.c_ref), custom_call_target="tpu_custom_call" | custom-call | tf_op jit(solution)/shard_map/pallas_call | solution.py:428

commit v4 on v3

--- a/solution.py
+++ b/solution.py
@@ -95,6 +95,9 @@
     def plane(d):
         return lax.rem(x + d[0], X) * Y + lax.rem(y + d[1], Y)
 
+    def others(n, own):
+        return [jnp.where(own <= i, i + 1, i) for i in range(n - 1)]
+
     def signal(sem, dev, core):
         pl.semaphore_signal(sem, inc=1, device_id=(dev, core), device_id_type=MESH)
 
@@ -140,7 +143,7 @@
         for d in z_order:
             send(xy * Z + zline(d))
 
-    first, second = xy_order[:len(xy_order) // 2], xy_order[len(xy_order) // 2:]
+    first, second = xy_order[:11], xy_order[11:]
 
     def send_bnd(p):
         remote(s1.at[p], br.at[r], 3, p, g).start()
@@ -300,8 +303,8 @@
     w_sib.start()
     w_sib.wait_recv()
     wp[1] = total + wsib[...]
-    for d in z_order:
-        remote(wp.at[1], wz.at[z], 11, xy * Z + zline(d), g).start()
+    for p in others(Z, z):
+        remote(wp.at[1], wz.at[z], 11, xy * Z + p, g).start()
     pltpu.make_async_copy(wp.at[1], wz.at[z], rsem.at[11]).start()
 
     each(second, send_back)
@@ -314,8 +317,8 @@
     for i in range(1, XY):
         total += gx[i]
     gp[...] = total.reshape(Z, 4, F)
-    for d in z_order:
-        remote(gp.at[zline(d)], gz.at[z], 10, xy * Z + zline(d), g).start()
+    for p in others(Z, z):
+        remote(gp.at[p], gz.at[z], 10, xy * Z + p, g).start()
     pltpu.make_async_copy(gp.at[z], gz.at[z], rsem.at[10]).start()
 
     wait_recv(wz, 11)
@@ -324,8 +327,8 @@
         total += wz[i]
     wsum[...] = total
 
-    for d in xy_order:
-        remote(wsum, wall.at[xy], 13, plane(d) * Z + z, g).start()
+    for p in others(XY, xy):
+        remote(wsum, wall.at[xy], 13, p * Z + z, g).start()
     pltpu.make_async_copy(wsum, wall.at[xy], rsem.at[13]).start()
 
     loads["srows_v"].wait()

time: 41.3 us -> 40.6 us (0.983)
  Pallas kernels: 40.6 us -> 39.8 us
    pallas_call x1, Pallas kernels: 39.6 us -> 38.9 us  [shards(): pl.pallas_call(functools.partial(kernel, X, Y, Z), out_shape=(pltpu.VMEM(...]
where the time goes in v4:
time: 40.6 us; the launch traced here: 40.5 us
  Pallas kernels  39.8 us (98%)
  between operations  0.64 us (2%)
    pallas_call x1, Pallas kernels, shards(): pl.pallas_call(functools.partial(kernel, X, Y, Z), out_shape=(pltpu.VMEM(...  38.9 us
    pallas_call x1, Pallas kernels, shards(): pl.pallas_call(write_out, out_shape=(jax.ShapeDtypeStruct((N, H), F32), j...  0.95 us

profile of v4, /device:TPU:1, one launch (start us, length us, event | category | flops | bytes accessed | tf_op | source)
XLA Modules:
  0.0 40.5 jit_solution(1286546787627441098)
XLA Ops:
  0.6 38.9 %shard_map.130 = (f32[512,256]{1,0:T(8,128)S(1)}, f32[128,256]{1,0:T(8,128)S(1)}, f32[512,128]{1,0:T(8,128)S(1)}) custom-call(f32[512,128]{1,0:T(8,128)} %feat_h.1, f32[128,256]{1,0:T(8,128)} %w_h.1, f32[1,256]{1,0:T(1,128)} %bitcast.9, f32[512,256]{1,0:T(8,128)} %cot_h.1, f32[512,256]{1,0:T(8,128)} %lv_h.1, s32[4,8]{1,0:T(4,128)} %bitcast.7, ...), custom_call_target="tpu_custom_call" | custom-call | tf_op jit(solution)/shard_map/pallas_call | solution.py:417
  39.5 0.9 %shard_map.131 = (f32[512,256]{1,0:T(8,128)}, f32[128,256]{1,0:T(8,128)}, f32[512,128]{1,0:T(8,128)}) custom-call(f32[512,256]{1,0:T(8,128)S(1)} %get-tuple-element.6.a_ref, f32[128,256]{1,0:T(8,128)S(1)} %get-tuple-element.7.b_ref, f32[512,128]{1,0:T(8,128)S(1)} %get-tuple-element.8.c_ref), custom_call_target="tpu_custom_call" | custom-call | tf_op jit(solution)/shard_map/pallas_call | solution.py:431

commit v5 on v4

--- a/solution.py
+++ b/solution.py
@@ -248,21 +248,25 @@
     loads["b"].wait()
     loads["cot"].wait()
     H = w.shape[1]
-    step = 128
+    step = N // 4
     wsplit = wpair[...]
-    for c in range(N // step):
+    wterm = jnp.zeros((F, H), F32)
+    for c in range(4):
         rows = pl.ds(c * step, step)
-        high, low = split(agg[rows, :])
+        part = agg[rows, :]
+        high, low = split(part)
         both = mm(high, wsplit)
         v = both[:, :H] + both[:, H:] + mm(low, wsplit[:, :H]) + b[...]
         sq = v * v
         t = jnp.tanh(C0 * (v + C1 * (sq * v)))
         act_o[rows, :] = 0.5 * v * (1.0 + t)
         slope = 0.5 * (1.0 + t) + 0.5 * v * (1.0 - t * t) * (C0 * (1.0 + 3.0 * C1 * sq))
-        prg[rows, :] = cot[rows, :] * slope
-    ahigh, alow = split(agg[...].T)
-    wh, wl = split(prg[...])
-    wterm = mm(ahigh, wh) + mm(ahigh, wl) + mm(alow, wh)
+        grad = cot[rows, :] * slope
+        prg[rows, :] = grad
+        ahigh, alow = split(part.T)
+        wh, wl = split(grad)
+        wterm += mm(ahigh, wh) + mm(ahigh, wl) + mm(alow, wh)
+
     ws[...] = jnp.concatenate([wterm[:, :F], wterm[:, F:]], axis=0).reshape(ws.shape)
     for d in xy_order:
         remote(ws.at[plane(d)], wx.at[xy], 8, plane(d) * Z + z, g).start()

time: 40.6 us -> 41 us (level)
  Pallas kernels: 39.8 us -> 40.3 us
where the time goes in v5:
time: 41 us; the launch traced here: 40.9 us
  Pallas kernels  40.3 us (98%)
  between operations  0.64 us (2%)
    pallas_call x1, Pallas kernels, shards(): pl.pallas_call(functools.partial(kernel, X, Y, Z), out_shape=(pltpu.VMEM(...  39.3 us
    pallas_call x1, Pallas kernels, shards(): pl.pallas_call(write_out, out_shape=(jax.ShapeDtypeStruct((N, H), F32), j...  0.95 us

profile of v5, /device:TPU:1, one launch (start us, length us, event | category | flops | bytes accessed | tf_op | source)
XLA Modules:
  0.0 40.9 jit_solution(17343410577560461018)
XLA Ops:
  0.6 39.3 %shard_map.130 = (f32[512,256]{1,0:T(8,128)S(1)}, f32[128,256]{1,0:T(8,128)S(1)}, f32[512,128]{1,0:T(8,128)S(1)}) custom-call(f32[512,128]{1,0:T(8,128)} %feat_h.1, f32[128,256]{1,0:T(8,128)} %w_h.1, f32[1,256]{1,0:T(1,128)} %bitcast.9, f32[512,256]{1,0:T(8,128)} %cot_h.1, f32[512,256]{1,0:T(8,128)} %lv_h.1, s32[4,8]{1,0:T(4,128)} %bitcast.7, ...), custom_call_target="tpu_custom_call" | custom-call | tf_op jit(solution)/shard_map/pallas_call | solution.py:421
  39.9 0.9 %shard_map.131 = (f32[512,256]{1,0:T(8,128)}, f32[128,256]{1,0:T(8,128)}, f32[512,128]{1,0:T(8,128)}) custom-call(f32[512,256]{1,0:T(8,128)S(1)} %get-tuple-element.6.a_ref, f32[128,256]{1,0:T(8,128)S(1)} %get-tuple-element.7.b_ref, f32[512,128]{1,0:T(8,128)S(1)} %get-tuple-element.8.c_ref), custom_call_target="tpu_custom_call" | custom-call | tf_op jit(solution)/shard_map/pallas_call | solution.py:435

commit v6 on v4

--- a/solution.py
+++ b/solution.py
@@ -79,8 +79,6 @@
         ("cot", cot_h, cot), ("srows_v", srows_h, srows_v),
     ]):
         arrays[name] = (src, dst, i)
-    load("srows", "hrows", "feat")
-
     barrier = pltpu.get_barrier_semaphore()
     x = xy // Y
     y = lax.rem(xy, Y)
@@ -106,17 +104,18 @@
     for d in xy_order:
         signal(barrier, plane(d) * Z + z, g)
     signal(barrier, r, 1 - g)
+    load("hrows", "feat", "srows")
     load("lcols", "lcount", "lv", "w", "b", "srows_v")
+
+    pl.semaphore_wait(barrier, (Z - 1) + (XY - 1) + 1)
+
+    for d in z_order:
+        signal(plane_sem.at[z], xy * Z + zline(d), g)
 
     loads["hrows"].wait()
     loads["feat"].wait()
     for j in range(4):
         hown[pl.ds(j, 1), :] = feat[pl.ds(hrows[0, j], 1), :]
-
-    pl.semaphore_wait(barrier, (Z - 1) + (XY - 1) + 1)
-
-    for d in z_order:
-        signal(plane_sem.at[z], xy * Z + zline(d), g)
 
     def remote(src, dst, k, dev, core):
         return pltpu.make_async_remote_copy(

time: 40.6 us -> 40.6 us (level)
  no operation moved by 1% of the time
where the time goes in v6:
time: 40.6 us
  Pallas kernels  39.9 us (98%)
  between operations  0.64 us (2%)
    pallas_call x1, Pallas kernels, shards(): pl.pallas_call(functools.partial(kernel, X, Y, Z), out_shape=(pltpu.VMEM(...  39 us
    pallas_call x1, Pallas kernels, shards(): pl.pallas_call(write_out, out_shape=(jax.ShapeDtypeStruct((N, H), F32), j...  0.95 us

profile of v6, /device:TPU:1, one launch (start us, length us, event | category | flops | bytes accessed | tf_op | source)
XLA Modules:
  0.0 40.6 jit_solution(15123470090916778367)
XLA Ops:
  0.6 39.0 %shard_map.130 = (f32[512,256]{1,0:T(8,128)S(1)}, f32[128,256]{1,0:T(8,128)S(1)}, f32[512,128]{1,0:T(8,128)S(1)}) custom-call(f32[512,128]{1,0:T(8,128)} %feat_h.1, f32[128,256]{1,0:T(8,128)} %w_h.1, f32[1,256]{1,0:T(1,128)} %bitcast.9, f32[512,256]{1,0:T(8,128)} %cot_h.1, f32[512,256]{1,0:T(8,128)} %lv_h.1, s32[4,8]{1,0:T(4,128)} %bitcast.7, ...), custom_call_target="tpu_custom_call" | custom-call | tf_op jit(solution)/shard_map/pallas_call | solution.py:416
  39.6 0.9 %shard_map.131 = (f32[512,256]{1,0:T(8,128)}, f32[128,256]{1,0:T(8,128)}, f32[512,128]{1,0:T(8,128)}) custom-call(f32[512,256]{1,0:T(8,128)S(1)} %get-tuple-element.6.a_ref, f32[128,256]{1,0:T(8,128)S(1)} %get-tuple-element.7.b_ref, f32[512,128]{1,0:T(8,128)S(1)} %get-tuple-element.8.c_ref), custom_call_target="tpu_custom_call" | custom-call | tf_op jit(solution)/shard_map/pallas_call | solution.py:430
